TPU v7x, 32 devices: a whole 2x2x4 slice. The times are simulated.
32 devices in a mesh: grp: 4 (over y, x), patch: 8 (over z, core).
Axes of the slice: x: 2, y: 2, z: 4, core: 2. Of those that a mesh axis runs over, the one named last changes fastest.
Arguments:
- fine_latent: bfloat16 [4096, 512], P(('grp', 'patch')), may hold values from -6 to 6
- edge_latent: bfloat16 [16384, 512], P(('grp', 'patch')), may hold values from -13 to 13
- coarse_latent: bfloat16 [256, 512], replicated, may hold values from -6 to 6
- first_proj: bfloat16 [1536, 512], P('patch'), may hold values from -0.15625 to 0.15625
- second_proj: bfloat16 [512, 512], P('patch'), may hold values from -1 to 1
- senders: int32 [16384], P(('grp', 'patch')), may hold values from 0 to 511, as said below
- receivers: int32 [16384], P(('grp', 'patch')), may hold values from 0 to 127
- block_counts: int32 [128], P(('grp', 'patch')), may hold values from 64 to 128, as said below
- send_rows: int32 [128, 32], P(('grp', 'patch')), may hold values from 0 to 127, as said below
- cot_edges: bfloat16 [16384, 512], P(('grp', 'patch')), may hold values from -6 to 6
- cot_fine: bfloat16 [4096, 512], P(('grp', 'patch')), may hold values from -6 to 6
Outputs:
- new_edges: bfloat16 [16384, 512], P(('grp', 'patch'))
- fine_messages: bfloat16 [4096, 512], P(('grp', 'patch'))
- grad_edges: bfloat16 [16384, 512], P(('grp', 'patch'))
- grad_fine: bfloat16 [4096, 512], P(('grp', 'patch'))
- grad_coarse: float32 [256, 512], P('patch')
- grad_first: float32 [1536, 512], P('patch')
- grad_second: float32 [512, 512], P('patch')
Inputs may be any that keep to these rules, and one draw needn't show every extreme that they name: `senders`: A sender below 128 is a local fine node, the next 128 rows are the received rows in the table's order, the last 256 are coarse nodes. `block_counts`: the live edges of a block of 128 slots are its first ones; some block holds 128 and some 64. `send_rows`: each list holds 32 distinct local rows.
All inputs are finite; a program needn't handle non-finite values.
Results may differ from a plain program's by a relative error of at most 0.015.
Values may be sent and summed in bfloat16 or wider, within the bound.
A program may use at most 64 MiB of HBM per device.

v0:
```python
import jax
import jax.numpy as jnp
from jax import lax
from jax.sharding import PartitionSpec as P

norm_eps = 1e-05


def shifted(shard, axis, by):
    devices = lax.axis_size(axis)
    return lax.ppermute(shard, axis, [(i, (i + by) % devices) for i in range(devices)])


def pass_lon(buffer, offset):
    return shifted(buffer, "patch", offset)


def pass_lat(buffer, offset):
    return shifted(buffer, "grp", offset)


def neighbours(blocks):
    return jnp.concatenate(
        [
            pass_lon(blocks[1], 1),
            pass_lon(blocks[0], -1),
            pass_lat(blocks[3], 1),
            pass_lat(blocks[2], -1),
        ],
        axis=0,
    )


def row_sums(first_part, second_part):
    return (
        lax.psum_scatter(
            first_part.astype(jnp.bfloat16), "patch", scatter_dimension=0, tiled=True
        ).astype(jnp.float32),
        lax.psum_scatter(
            second_part.astype(jnp.bfloat16), "patch", scatter_dimension=0, tiled=True
        ).astype(jnp.float32),
    )


def coarse_whole(coarse_part):
    coarse_sum = lax.psum(coarse_part, ("grp", "patch"))
    share_rows = coarse_part.shape[0] // lax.axis_size("patch")
    return lax.dynamic_slice_in_dim(coarse_sum, lax.axis_index("patch") * share_rows, share_rows, 0)


def on_device(
    fine_latent,
    edge_latent,
    coarse_latent,
    first_proj,
    second_proj,
    senders,
    receivers,
    block_counts,
    send_rows,
    cot_edges,
    cot_fine,
):
    node_count = fine_latent.shape[0]
    edge_count = edge_latent.shape[0]
    feat_width = edge_latent.shape[1]
    list_rows = send_rows.shape[1]
    halo_count = 4 * list_rows
    outgoing = jnp.take(fine_latent, send_rows, axis=0)
    node_table = jnp.concatenate([fine_latent, neighbours(outgoing), coarse_latent], axis=0)
    first_full, second_full = (
        lax.all_gather(first_proj, "patch", axis=0, tiled=True),
        lax.all_gather(second_proj, "patch", axis=0, tiled=True),
    )
    positions = lax.iota(jnp.int32, 128)
    live_mask = (
        (positions[None, :] < block_counts[:, None])
        .reshape(edge_count)
        .astype(jnp.float32)[:, None]
    )
    joined = jnp.concatenate(
        [
            edge_latent,
            jnp.take(node_table, senders, axis=0),
            jnp.take(fine_latent, receivers, axis=0),
        ],
        axis=1,
    )
    pre_act = jnp.dot(joined, first_full, preferred_element_type=jnp.float32)
    hidden = jax.nn.silu(pre_act).astype(jnp.bfloat16)
    outer_proj = jnp.dot(hidden, second_full, preferred_element_type=jnp.float32)
    centre = outer_proj - jnp.mean(outer_proj, axis=1, keepdims=True)
    norm_scale = jnp.sqrt(jnp.mean(centre * centre, axis=1, keepdims=True) + norm_eps)
    normed = centre / norm_scale
    message = live_mask * normed
    new_edges = (edge_latent.astype(jnp.float32) + message).astype(jnp.bfloat16)
    fine_messages = jax.ops.segment_sum(message, receivers, num_segments=node_count).astype(
        jnp.bfloat16
    )
    upstream = live_mask * (
        cot_edges.astype(jnp.float32) + jnp.take(cot_fine, receivers, axis=0).astype(jnp.float32)
    )
    d_outer = (
        (
            upstream
            - jnp.mean(upstream, axis=1, keepdims=True)
            - normed * jnp.mean(upstream * normed, axis=1, keepdims=True)
        )
        / norm_scale
    ).astype(jnp.bfloat16)
    d_hidden = lax.dot_general(
        d_outer, second_full, (((1,), (1,)), ((), ())), preferred_element_type=jnp.float32
    )
    gate_sig = jax.nn.sigmoid(pre_act)
    d_pre = (d_hidden * gate_sig * (1.0 + pre_act * (1.0 - gate_sig))).astype(jnp.bfloat16)
    d_joined = lax.dot_general(
        d_pre, first_full, (((1,), (1,)), ((), ())), preferred_element_type=jnp.float32
    )
    grad_edges = (cot_edges.astype(jnp.float32) + d_joined[:, :feat_width]).astype(jnp.bfloat16)
    d_table = jax.ops.segment_sum(
        d_joined[:, feat_width : 2 * feat_width], senders, num_segments=node_table.shape[0]
    )
    local_grad = d_table[:node_count] + jax.ops.segment_sum(
        d_joined[:, 2 * feat_width :], receivers, num_segments=node_count
    )
    halo_back = d_table[node_count : node_count + halo_count].astype(jnp.bfloat16)
    returned = neighbours(halo_back.reshape(4, list_rows, feat_width)).astype(jnp.float32)
    added = jax.ops.segment_sum(returned, send_rows.reshape(halo_count), num_segments=node_count)
    grad_fine = (local_grad + added).astype(jnp.bfloat16)
    coarse_part = d_table[node_count + halo_count :]
    first_part = lax.dot_general(
        joined, d_pre, (((0,), (0,)), ((), ())), preferred_element_type=jnp.float32
    )
    second_part = lax.dot_general(
        hidden, d_outer, (((0,), (0,)), ((), ())), preferred_element_type=jnp.float32
    )
    first_share, second_share = row_sums(first_part, second_part)
    grad_coarse = coarse_whole(coarse_part)
    grad_first, grad_second = (
        lax.psum(first_share.astype(jnp.bfloat16), "grp").astype(jnp.float32),
        lax.psum(second_share.astype(jnp.bfloat16), "grp").astype(jnp.float32),
    )
    return (new_edges, fine_messages, grad_edges, grad_fine, grad_coarse, grad_first, grad_second)


def solution(mesh):
    placed = (
        P(("grp", "patch"), None),
        P(("grp", "patch"), None),
        P(),
        P("patch", None),
        P("patch", None),
        P(("grp", "patch")),
        P(("grp", "patch")),
        P(("grp", "patch")),
        P(("grp", "patch"), None),
        P(("grp", "patch"), None),
        P(("grp", "patch"), None),
    )
    return jax.shard_map(
        on_device,
        mesh=mesh,
        in_specs=placed,
        out_specs=(
            P(("grp", "patch"), None),
            P(("grp", "patch"), None),
            P(("grp", "patch"), None),
            P(("grp", "patch"), None),
            P("patch", None),
            P("patch", None),
            P("patch", None),
        ),
        check_vma=False,
    )
```

profile of v0, /device:TPU:0, one launch (start us, length us, event | category | flops | bytes accessed | tf_op | source)
XLA Modules:
  0.0 305.3 jit_solution(14776376052635775314)
XLA Ops:
  7.2 0.7 all-gather.2.cloned.1.call-update
  8.0 0.7 compare_and_fusion.1
  8.7 0.7 compare_select_fusion.1
  9.4 0.7 compare_select_fusion
  10.1 1.8 gather_fusion
  12.0 0.7 slice_bitcast_fusion
  12.7 3.9 %collective-permute-start.3 = (bf16[32,512]{1,0:T(8,128)(2,1)}, bf16[32,512]{1,0:T(8,128)(2,1)S(1)}, u32[]{:S(2)}, u32[]{:S(2)}) collective-permute-start(bf16[32,512]{1,0:T(8,128)(2,1)} %get-tuple-element.33), channel_id=1, source_target_pairs={{0,24},{8,0},{16,8},{24,16},{1,25},{9,1},{17,9},{25,17},{2,26},{10... | collective-permute-start | bytes 98312 | tf_op jit(solution)/shard_map/ppermute | solution.py:11
  16.6 2.8 collective-permute-start.1
  19.4 2.0 gather_fusion.2
  21.4 0.5 compare_and_fusion.2
  22.0 16.9 %all_gather.7 = bf16[512,512]{1,0:T(8,128)(2,1)S(1)} all-gather(bf16[64,512]{1,0:T(8,128)(2,1)S(1)} %copy-done.13), channel_id=1, replica_groups=mesh['grp'=4,'patch'=8] {'patch'}, dimensions={0}, use_global_device_ids=true | all-gather | bytes 589824 | tf_op jit(solution)/shard_map/all_gather | solution.py:73
  39.0 0.9 broadcast_select_fusion
  40.1 2.0 gather_fusion.3
  42.7 1.0 constant_dynamic-update-slice_fusion
  43.6 2.0 gather_fusion.1
  45.8 2.9 fusion.9
  48.7 0.6 fusion.27
  49.5 0.4 fusion.8
  49.9 1.7 add_convert_fusion
  51.6 1.3 convolution_convert_fusion.1
  53.1 2.0 fusion.1
  55.1 0.8 copy-done.6
  55.9 2.2 convolution_convert_fusion
  58.3 0.4 copy-done.14
  58.8 2.6 fusion.28
  61.5 4.6 %scatter_custom_fusion.1 = f32[512,512]{1,0:T(8,128)} fusion(s32[512]{0:T(512)S(1)} %copy-done.15, f32[512,1536]{1,0:T(8,128)S(1)} %fusion.28, f32[]{:T(128)} %constant.47.clone.1), kind=kCustom, calls=%fused_computation.20 | custom fusion | flops 262144 | bytes 2097156 | tf_op jit(solution)/shard_map/scatter-add | solution.py:120
  66.1 1.9 slice.82
  68.0 1.4 convert.4
  69.6 1.3 copy.31
  70.9 0.6 fusion.26
  71.5 0.3 collective-permute-start.4
  71.9 2.7 collective-permute-start.7
  74.6 2.9 collective-permute-start.5
  77.6 2.5 fusion.3
  80.1 2.0 copy.29
  82.1 3.8 %scatter_custom_fusion.2 = f32[128,512]{1,0:T(8,128)S(1)} fusion(f32[128,512]{1,0:T(8,128)S(1)} %slice-done.1, s32[512]{0:T(512)S(1)} %copy-done.16, f32[512,1536]{1,0:T(8,128)S(1)} %copy-done.3), kind=kCustom, calls=%fused_computation.18 | custom fusion | flops 262144 | bytes 1310720 | tf_op jit(solution)/shard_map/scatter-add | solution.py:123
  85.9 2.1 copy.30
  88.1 0.3 copy.25
  88.4 3.6 %scatter_custom_fusion = f32[128,512]{1,0:T(8,128)S(1)} fusion(s32[512]{0:T(512)S(1)} %copy-done.16, f32[512,512]{1,0:T(8,128)S(1)} %copy.25, f32[]{:T(128)} %constant.47.clone.1), kind=kCustom, calls=%fused_computation.47 | custom fusion | flops 262144 | bytes 262148 | tf_op jit(solution)/shard_map/scatter-add | solution.py:97
  92.1 0.7 convert_element_type.66
  92.8 1.7 scatter_custom_fusion.3
  94.5 24.1 %reduce-scatter.3.cloned.1.call-done = bf16[192,512]{1,0:T(8,128)(2,1)} async-done(((bf16[1536,512]{1,0:T(8,128)(2,1)}), bf16[192,512]{1,0:T(8,128)(2,1)}) %reduce-scatter.3.cloned.1.call-update) | async-done | bytes 196624 | tf_op jit(solution)/shard_map/reduce_scatter | solution.py:36
  118.6 0.7 add_convert_fusion.1
  119.3 131.4 %all-reduce.4.cloned.1.call-done = f32[256,512]{1,0:T(8,128)} async-done(((f32[256,512]{1,0:T(8,128)}), f32[256,512]{1,0:T(8,128)}) %all-reduce.4.cloned.1.call-update) | async-done | bytes 524304 | tf_op jit(solution)/shard_map/psum | solution.py:46
  250.7 1.5 constant_dynamic-slice_fusion
  252.2 43.4 %all-reduce.6.cloned.1.call-done = (bf16[192,512]{1,0:T(8,128)(2,1)}, bf16[64,512]{1,0:T(8,128)(2,1)}) async-done(((bf16[192,512]{1,0:T(8,128)(2,1)}, bf16[64,512]{1,0:T(8,128)(2,1)}), (bf16[192,512]{1,0:T(8,128)(2,1)}, bf16[64,512]{1,0:T(8,128)(2,1)})) %all-reduce.6.cloned.1.call-update) | async-done | bytes 262160 | tf_op jit(solution)/shard_map/psum | solution.py:140
  295.6 1.5 convert_element_type.77
  297.1 1.7 convert_element_type.75
  (90 shorter events, 2.1 us)
Async XLA Ops:
  7.2 32.9 %copy-start = (bf16[128,512]{1,0:T(8,128)(2,1)S(1)}, bf16[128,512]{1,0:T(8,128)(2,1)}, u32[]{:S(2)}) copy-start(bf16[128,512]{1,0:T(8,128)(2,1)} %param.23) | copy-start | bytes 393220
  7.2 12.2 %copy-start.1 = (bf16[128,512]{1,0:T(8,128)(2,1)S(1)}, bf16[128,512]{1,0:T(8,128)(2,1)}, u32[]{:S(2)}) copy-start(bf16[128,512]{1,0:T(8,128)(2,1)} %param.13) | copy-start | bytes 393220
  7.2 38.6 %all-gather.2.cloned.1.call-start = ((), (), s32[]{:S(2)}) async-start(), calls=%async_computation.2 | async-start | bytes 1769472 | tf_op jit(solution)/shard_map/all_gather | solution.py:72
  7.9 86.6 %reduce-scatter.5.cloned.1.call-start = ((), (), s32[]{:S(2)}) async-start(), calls=%async_computation.5 | async-start | bytes 589824 | tf_op jit(solution)/shard_map/reduce_scatter | solution.py:39
  12.7 30.0 %collective-permute-start.3 = (bf16[32,512]{1,0:T(8,128)(2,1)}, bf16[32,512]{1,0:T(8,128)(2,1)S(1)}, u32[]{:S(2)}, u32[]{:S(2)}) collective-permute-start(bf16[32,512]{1,0:T(8,128)(2,1)} %get-tuple-element.33), channel_id=1, source_target_pairs={{0,24},{8,0},{16,8},{24,16},{1,25},{9,1},{17,9},{25,17},{2,26},{10... | collective-permute-start | bytes 98312 | tf_op jit(solution)/shard_map/ppermute | solution.py:11
  16.6 26.0 %collective-permute-start.2 = (bf16[32,512]{1,0:T(8,128)(2,1)}, bf16[32,512]{1,0:T(8,128)(2,1)S(1)}, u32[]{:S(2)}, u32[]{:S(2)}) collective-permute-start(bf16[32,512]{1,0:T(8,128)(2,1)} %get-tuple-element.34), channel_id=1, source_target_pairs={{0,8},{8,16},{16,24},{24,0},{1,9},{9,17},{17,25},{25,1},{2,10},{10... | collective-permute-start | bytes 98312 | tf_op jit(solution)/shard_map/ppermute | solution.py:11
  16.6 26.0 %collective-permute-start.1 = (bf16[32,512]{1,0:T(8,128)(2,1)}, bf16[32,512]{1,0:T(8,128)(2,1)S(1)}, u32[]{:S(2)}, u32[]{:S(2)}) collective-permute-start(bf16[32,512]{1,0:T(8,128)(2,1)} %get-tuple-element.35), channel_id=1, source_target_pairs={{0,7},{1,0},{2,1},{3,2},{4,3},{5,4},{6,5},{7,6},{8,15},{9,8},{10,9... | collective-permute-start | bytes 98312 | tf_op jit(solution)/shard_map/ppermute | solution.py:11
  19.3 23.2 %collective-permute-start = (bf16[32,512]{1,0:T(8,128)(2,1)}, bf16[32,512]{1,0:T(8,128)(2,1)S(1)}, u32[]{:S(2)}, u32[]{:S(2)}) collective-permute-start(bf16[32,512]{1,0:T(8,128)(2,1)} %get-tuple-element.36), channel_id=1, source_target_pairs={{0,1},{1,2},{2,3},{3,4},{4,5},{5,6},{6,7},{7,0},{8,9},{9,10},{10,1... | collective-permute-start | bytes 98312 | tf_op jit(solution)/shard_map/ppermute | solution.py:11
  19.3 2.0 copy-start.16
  19.3 2.1 copy-start.15
  19.3 2.6 copy-start.20
  19.4 2.7 copy-start.13
  21.4 18.5 %copy-start.7 = (bf16[512,512]{1,0:T(8,128)(2,1)S(1)}, bf16[512,512]{1,0:T(8,128)(2,1)}, u32[]{:S(2)}) copy-start(bf16[512,512]{1,0:T(8,128)(2,1)} %param.22) | copy-start | bytes 1572868
  21.4 17.5 %copy-start.17 = (pred[512]{0:T(512)(128)(4,1)}, pred[512]{0:T(512)(128)(4,1)S(1)}, u32[]{:S(2)}) copy-start(pred[512]{0:T(512)(128)(4,1)S(1)} %compare_and_fusion) | copy-start | bytes 1540
  40.1 9.8 %copy-start.4 = (bf16[512,512]{0,1:T(8,128)(2,1)}, bf16[512,512]{0,1:T(8,128)(2,1)S(1)}, u32[]{:S(2)}) copy-start(bf16[512,512]{0,1:T(8,128)(2,1)S(1)} %copy.26) | copy-start | bytes 1572868
  40.1 2.2 copy-start.8
  43.6 2.0 copy-start.19
  45.8 2.9 copy-start.11
  48.7 2.9 copy-start.21
  48.7 0.8 copy-start.18
  53.0 2.9 copy-start.9
  53.0 2.9 copy-start.10
  53.0 2.9 copy-start.12
  53.0 65.6 %reduce-scatter.3.cloned.1.call-start = ((), (), s32[]{:S(2)}) async-start(), calls=%async_computation.4 | async-start | bytes 1769472 | tf_op jit(solution)/shard_map/reduce_scatter | solution.py:36
  55.1 0.8 copy-start.6
  58.1 0.7 copy-start.14
  58.1 192.6 %all-reduce.4.cloned.1.call-start = ((), (), s32[]{:S(2)}) async-start(), calls=%async_computation.3 | async-start | bytes 1048576 | tf_op jit(solution)/shard_map/psum | solution.py:46
  61.4 4.7 %copy-start.2 = (f32[512,1536]{1,0:T(8,128)}, f32[512,1536]{1,0:T(8,128)S(1)}, u32[]{:S(2)}) copy-start(f32[512,1536]{1,0:T(8,128)S(1)} %fusion.28) | copy-start | bytes 9437188
  68.0 1.5 slice-start
  71.5 21.2 %collective-permute-start.4 = (bf16[32,512]{1,0:T(8,128)(2,1)}, bf16[32,512]{1,0:T(8,128)(2,1)}, u32[]{:S(2)}, u32[]{:S(2)}) collective-permute-start(bf16[32,512]{1,0:T(8,128)(2,1)} %get-tuple-element.29), channel_id=1, source_target_pairs={{0,1},{1,2},{2,3},{3,4},{4,5},{5,6},{6,7},{7,0},{8,9},{9,10},{10,1... | collective-permute-start | bytes 98312 | tf_op jit(solution)/shard_map/ppermute | solution.py:11
  71.9 20.9 %collective-permute-start.7 = (bf16[32,512]{1,0:T(8,128)(2,1)}, bf16[32,512]{1,0:T(8,128)(2,1)}, u32[]{:S(2)}, u32[]{:S(2)}) collective-permute-start(bf16[32,512]{1,0:T(8,128)(2,1)} %get-tuple-element.30), channel_id=1, source_target_pairs={{0,24},{8,0},{16,8},{24,16},{1,25},{9,1},{17,9},{25,17},{2,26},{10... | collective-permute-start | bytes 98312 | tf_op jit(solution)/shard_map/ppermute | solution.py:11
  74.6 18.1 %collective-permute-start.6 = (bf16[32,512]{1,0:T(8,128)(2,1)}, bf16[32,512]{1,0:T(8,128)(2,1)}, u32[]{:S(2)}, u32[]{:S(2)}) collective-permute-start(bf16[32,512]{1,0:T(8,128)(2,1)} %get-tuple-element.31), channel_id=1, source_target_pairs={{0,8},{8,16},{16,24},{24,0},{1,9},{9,17},{17,25},{25,1},{2,10},{10... | collective-permute-start | bytes 98312 | tf_op jit(solution)/shard_map/ppermute | solution.py:11
  74.6 18.2 %collective-permute-start.5 = (bf16[32,512]{1,0:T(8,128)(2,1)}, bf16[32,512]{1,0:T(8,128)(2,1)}, u32[]{:S(2)}, u32[]{:S(2)}) collective-permute-start(bf16[32,512]{1,0:T(8,128)(2,1)} %get-tuple-element.32), channel_id=1, source_target_pairs={{0,7},{1,0},{2,1},{3,2},{4,3},{5,4},{6,5},{7,6},{8,15},{9,8},{10,9... | collective-permute-start | bytes 98312 | tf_op jit(solution)/shard_map/ppermute | solution.py:11
  77.6 4.6 %copy-start.3 = (f32[512,1536]{1,0:T(8,128)S(1)}, f32[512,1536]{1,0:T(8,128)}, u32[]{:S(2)}) copy-start(f32[512,1536]{1,0:T(8,128)} %copy-done.2) | copy-start | bytes 9437188
  77.6 4.6 %slice-start.1 = ((f32[512,512]{1,0:T(8,128)}), f32[128,512]{1,0:T(8,128)S(1)}, s32[]{:S(2)}) async-start(f32[512,512]{1,0:T(8,128)} %scatter_custom_fusion.1), calls=%async_computation.8 | async-start | bytes 524288 | tf_op jit(solution)/shard_map/slice | solution.py:123
  77.6 218.0 %all-reduce.6.cloned.1.call-start = ((), (), s32[]{:S(2)}) async-start(), calls=%async_computation.6 | async-start | bytes 524288 | tf_op jit(solution)/shard_map/psum | solution.py:140
  85.9 2.1 copy-start.5
Sparse Core Ops, SparseCore 0:
  9.7 32.0 all-gather.1
  53.1 30.8 reduce-scatter.4
  86.4 32.1 reduce-scatter.2
  124.6 126.0 all-reduce.3
  253.5 42.0 all-reduce.5
where the time goes:
time: 306 us; the launch traced here: 305 us
  waiting for transfers between devices  200 us (65%)
  other arithmetic  28.3 us (9%)
  local copies, waits for them, and re-layouts  21.5 us (7%)
  blocking collectives  16.9 us (6%)
  between operations  14.3 us (5%)
  starting transfers between devices  13 us (4%)
  matrix products  11.6 us (4%)
    psum x1, waiting for transfers between devices, coarse_whole(): coarse_sum = lax.psum(coarse_part, ('grp', 'patch'))  131 us
    psum x1, waiting for transfers between devices, on_device(): lax.psum(first_share.astype(jnp.bfloat16), 'grp').astype(jnp.float32)  43.4 us
    reduce_scatter x1, waiting for transfers between devices, row_sums(): lax.psum_scatter(first_part.astype(jnp.bfloat16), 'patch', scatter_dimens...  24.1 us
    all_gather x1, blocking collectives, on_device(): lax.all_gather(second_proj, 'patch', axis=0, tiled=True)  16.9 us
    ppermute x8, starting transfers between devices, shifted(): lax.ppermute(shard, axis, [(i, (i + by) % devices) for i in range(devices)])  12.7 us
    unnamed x54, local copies, waits for them, and re-layouts  7.27 us
  transfers between devices with their start and end apart: 13, of which 3 were waited for; matrix products, arithmetic and copies ran while one was open for 16% of the time, Pallas kernels for 0%

commit v1 on v0

v1 whole, which is shorter than its diff:
```python
import functools

import jax
import jax.numpy as jnp
from jax import lax
from jax.experimental import pallas as pl
from jax.experimental.pallas import tpu as pltpu
from jax.sharding import PartitionSpec as P

norm_eps = 1e-05
LANES = 128
ROW_TILE = 16
EDGE_BLOCK = 256
PART_ROWS = 384
F32 = jnp.float32
BF16 = jnp.bfloat16


def dot(x, y):
    return jnp.dot(x, y, preferred_element_type=F32)


def dot_nt(x, y):
    return lax.dot_general(x, y, (((1,), (1,)), ((), ())), preferred_element_type=F32)


def dot_tn(x, y):
    return lax.dot_general(x, y, (((0,), (0,)), ((), ())), preferred_element_type=F32)


def picks(rows, index_row):
    where = lax.broadcasted_iota(jnp.int32, (rows, index_row.shape[1]), 0)
    return (where == index_row).astype(F32).astype(BF16)


def row_mean(x):
    return jnp.mean(x, axis=1, keepdims=True)


def kernel(
    groups,
    patches,
    counts_ref,
    fine_ref,
    edge_ref,
    coarse_ref,
    first_ref,
    second_ref,
    send_idx_ref,
    recv_idx_ref,
    list_idx_ref,
    cot_edge_ref,
    cot_fine_ref,
    new_edges_ref,
    fine_msg_ref,
    grad_edges_ref,
    grad_fine_ref,
    grad_coarse_ref,
    grad_first_ref,
    grad_second_ref,
    weights,
    outgoing,
    table,
    pick_send,
    pick_recv,
    joined,
    hidden,
    d_outer_all,
    d_pre_all,
    message_all,
    d_send_all,
    d_recv_all,
    halo_back,
    returned,
    parts,
    from_core,
    chip_sum,
    from_grp,
    plane_sum,
    from_z,
    whole_sum,
    from_far,
    result,
    w_z_sems,
    w_grp_sems,
    w_core_sems,
    halo_sems,
    back_sems,
    core_sems,
    grp_sems,
    z_sems,
    far_sems,
    result_sems,
):
    a = lax.axis_index("grp")
    b = lax.axis_index("patch")
    z = b // 2
    c = b % 2
    chips = patches // 2
    width = fine_ref.shape[1]
    blocks = width // LANES
    k = a % blocks
    base = a - k
    far_count = groups // blocks
    first_rows = first_ref.shape[0]
    second_rows = second_ref.shape[0]
    coarse_rows = grad_coarse_ref.shape[0]
    node_count = fine_ref.shape[0]
    halo_count = list_idx_ref.shape[1]
    list_rows = halo_count // 4
    edge_count = edge_ref.shape[0]
    weight_rows = first_rows + second_rows
    part_rows = parts.shape[1]
    sibling = (a, 2 * z + 1 - c)
    pending = []

    def send(src, dst, sems, at, device):
        copy = pltpu.make_async_remote_copy(
            src_ref=src,
            dst_ref=dst,
            send_sem=sems.at[(0,) + at],
            recv_sem=sems.at[(1,) + at],
            device_id=device,
            device_id_type=pl.DeviceIdType.MESH,
        )
        copy.start()
        pending.append(copy)
        return copy

    def columns(block):
        return pl.ds(pl.multiple_of(block * LANES, LANES), LANES)

    def chip_at(offset):
        return (z + offset + chips) % chips

    def peer(offset):
        return (base + (k + offset) % blocks, b)

    def exchange(src, dst, first_row, sems):
        routes = (
            (1, 0, (a, (b + 1) % patches)),
            (0, 1, (a, (b + patches - 1) % patches)),
            (3, 2, ((a + 1) % groups, b)),
            (2, 3, ((a + groups - 1) % groups, b)),
        )
        return [
            send(
                src.at[pl.ds(own * list_rows, list_rows), :],
                dst.at[pl.ds(first_row + slot * list_rows, list_rows), :],
                sems,
                (slot,),
                device,
            )
            for own, slot, device in routes
        ]

    barrier = pltpu.get_barrier_semaphore()
    for step in range(1, patches):
        pl.semaphore_signal(
            barrier, inc=1, device_id=(a, (b + step) % patches), device_id_type=pl.DeviceIdType.MESH
        )
    for step in range(1, groups):
        pl.semaphore_signal(
            barrier, inc=1, device_id=((a + step) % groups, b), device_id_type=pl.DeviceIdType.MESH
        )
    weights[b, :first_rows, :] = first_ref[...]
    weights[b, first_rows:, :] = second_ref[...]
    pick_list = picks(node_count, list_idx_ref[...])
    outgoing[...] = dot_tn(pick_list, fine_ref[...]).astype(BF16)
    pl.semaphore_wait(barrier, patches + groups - 2)

    along_z = [
        send(
            weights.at[b, :, columns(k)],
            weights.at[b, :, columns(k)],
            w_z_sems,
            (step - 1,),
            (a, 2 * chip_at(step) + c),
        )
        for step in range(1, chips)
    ]
    between = [send(weights.at[b], weights.at[b], w_core_sems, (0,), sibling)]
    halo = exchange(outgoing, table, node_count, halo_sems)
    table[:node_count, :] = fine_ref[...]
    table[node_count + halo_count :, :] = coarse_ref[...]
    over_grp = []
    for step in range(1, chips):
        along_z[step - 1].wait_recv()
        owner = 2 * chip_at(-step) + c
        over_grp.append(
            [
                send(
                    weights.at[owner, :, columns(k)],
                    weights.at[owner, :, columns(k)],
                    w_grp_sems,
                    (step - 1, offset - 1),
                    peer(offset),
                )
                for offset in range(1, blocks)
            ]
        )
    pick_send[...] = picks(table.shape[0], send_idx_ref[...])
    pick_recv[...] = picks(node_count, recv_idx_ref[...])
    joined[:, :width] = edge_ref[...]
    joined[:, 2 * width :] = dot_tn(pick_recv[...], fine_ref[...]).astype(BF16)
    for step in range(1, chips):
        for copy in over_grp[step - 1]:
            copy.wait_recv()
        owner = 2 * chip_at(-step) + c
        between.append(
            send(weights.at[owner], weights.at[owner], w_core_sems, (step,), sibling)
        )
    for copy in halo:
        copy.wait_recv()
    joined[:, width : 2 * width] = dot_tn(pick_send[...], table[...]).astype(BF16)
    for copy in between:
        copy.wait_recv()

    @pl.loop(0, edge_count // EDGE_BLOCK)
    def _(at):
        rows = pl.ds(pl.multiple_of(at * EDGE_BLOCK, EDGE_BLOCK), EDGE_BLOCK)
        first_full = weights[:, :first_rows, :].reshape(patches * first_rows, width)
        second_full = weights[:, first_rows:, :].reshape(patches * second_rows, width)
        pre_act = dot(joined[rows, :], first_full)
        gate_sig = 1.0 / (1.0 + jnp.exp(-pre_act))
        hid = (pre_act * gate_sig).astype(BF16)
        hidden[rows, :] = hid
        outer_proj = dot(hid, second_full)
        centre = outer_proj - row_mean(outer_proj)
        inv_scale = 1.0 / jnp.sqrt(row_mean(centre * centre) + norm_eps)
        normed = centre * inv_scale
        position = lax.broadcasted_iota(jnp.int32, (EDGE_BLOCK, 1), 0)
        per = EDGE_BLOCK // LANES
        bound = counts_ref[at * per]
        for extra in range(1, per):
            bound = jnp.where(
                position < extra * LANES, bound, counts_ref[at * per + extra] + extra * LANES
            )
        live = (position < bound).astype(F32)
        message = live * normed
        message_all[rows, :] = message.astype(BF16)
        new_edges_ref[rows, :] = (edge_ref[rows, :].astype(F32) + message).astype(BF16)
        cot = cot_edge_ref[rows, :].astype(F32)
        upstream = live * (cot + dot_tn(pick_recv[:, rows], cot_fine_ref[...]))
        d_outer = (
            (upstream - row_mean(upstream) - normed * row_mean(upstream * normed)) * inv_scale
        ).astype(BF16)
        d_outer_all[rows, :] = d_outer
        d_hidden = dot_nt(d_outer, second_full)
        d_pre = (d_hidden * gate_sig * (1.0 + pre_act * (1.0 - gate_sig))).astype(BF16)
        d_pre_all[rows, :] = d_pre
        grad_edges_ref[rows, :] = (cot + dot_nt(d_pre, first_full[:width])).astype(BF16)
        d_send_all[rows, :] = dot_nt(d_pre, first_full[width : 2 * width]).astype(BF16)
        d_recv_all[rows, :] = dot_nt(d_pre, first_full[2 * width :]).astype(BF16)

    halo_back[...] = dot(
        pick_send[node_count : node_count + halo_count, :], d_send_all[...]
    ).astype(BF16)
    back = exchange(halo_back, returned, 0, back_sems)
    coarse_part = dot(pick_send[node_count + halo_count :, :], d_send_all[...]).astype(BF16)
    second_part = dot_tn(hidden[...], d_outer_all[...]).astype(BF16)
    spare = part_rows - weight_rows - coarse_rows
    for at in range(patches):
        own_coarse = coarse_part[at * coarse_rows : (at + 1) * coarse_rows]
        if spare:
            own_coarse = jnp.concatenate([own_coarse, jnp.zeros((spare, width), BF16)], axis=0)
        parts[at, first_rows:weight_rows, :] = second_part[at * second_rows : (at + 1) * second_rows]
        parts[at, weight_rows:, :] = own_coarse
    to_core = []
    held = PART_ROWS // first_rows
    for at in range(patches // held):
        part = dot_tn(
            joined[:, at * PART_ROWS : (at + 1) * PART_ROWS], d_pre_all[...]
        ).astype(BF16)
        for place in range(held):
            parts[at * held + place, :first_rows, :] = part[
                place * first_rows : (place + 1) * first_rows
            ]
        for chip in range(at * held // 2, (at + 1) * held // 2):
            to_core.append(
                send(
                    parts.at[2 * chip + 1 - c], from_core.at[chip], core_sems, (chip,), sibling
                )
            )

    to_grp = []
    for chip in range(chips):
        to_core[chip].wait_recv()
        chip_sum[chip] = (parts[2 * chip + c].astype(F32) + from_core[chip].astype(F32)).astype(
            BF16
        )
        to_grp.append(
            [
                send(
                    chip_sum.at[chip, :, columns((k + offset) % blocks)],
                    from_grp.at[offset - 1, chip],
                    grp_sems,
                    (chip, offset - 1),
                    peer(offset),
                )
                for offset in range(1, blocks)
            ]
        )
    fine_msg_ref[...] = dot(pick_recv[...], message_all[...]).astype(BF16)
    local_grad = dot(pick_send[:node_count, :], d_send_all[...]) + dot(
        pick_recv[...], d_recv_all[...]
    )
    for copy in back:
        copy.wait_recv()
    grad_fine_ref[...] = (
        local_grad + dot(picks(node_count, list_idx_ref[...]), returned[...])
    ).astype(BF16)
    for chip in range(chips):
        total = chip_sum[chip, :, columns(k)].astype(F32)
        for offset in range(1, blocks):
            to_grp[chip][offset - 1].wait_recv()
            total = total + from_grp[offset - 1, chip].astype(F32)
        plane_sum[chip] = total.astype(BF16)
    to_z = [
        send(
            plane_sum.at[chip_at(step)],
            from_z.at[step - 1],
            z_sems,
            (step - 1,),
            (a, 2 * chip_at(step) + c),
        )
        for step in range(1, chips)
    ]
    total = plane_sum[z].astype(F32)
    for step in range(1, chips):
        to_z[step - 1].wait_recv()
        total = total + from_z[step - 1].astype(F32)
    whole_sum[...] = total.astype(BF16)
    if far_count > 1:
        to_far = [
            send(
                whole_sum,
                from_far.at[step - 1],
                far_sems,
                (step - 1,),
                ((a + step * blocks) % groups, b),
            )
            for step in range(1, far_count)
        ]
        for step in range(1, far_count):
            to_far[step - 1].wait_recv()
            total = total + from_far[step - 1].astype(F32)
    result[:, columns(k)] = total.astype(BF16)
    shares = [
        send(
            result.at[:, columns(k)],
            result.at[:, columns(k)],
            result_sems,
            (offset - 1,),
            peer(offset),
        )
        for offset in range(1, blocks)
    ]
    for copy in shares:
        copy.wait_recv()
    grad_first_ref[...] = result[:first_rows, :].astype(F32)
    grad_second_ref[...] = result[first_rows:weight_rows, :].astype(F32)
    grad_coarse_ref[...] = result[weight_rows:, :].astype(F32)[:coarse_rows]
    for copy in pending:
        copy.wait_send()


def on_device(
    groups,
    patches,
    fine_latent,
    edge_latent,
    coarse_latent,
    first_proj,
    second_proj,
    senders,
    receivers,
    block_counts,
    send_rows,
    cot_edges,
    cot_fine,
):
    node_count, width = fine_latent.shape
    edge_count = edge_latent.shape[0]
    halo_count = send_rows.size
    table_rows = node_count + halo_count + coarse_latent.shape[0]
    first_rows = first_proj.shape[0]
    second_rows = second_proj.shape[0]
    coarse_rows = coarse_latent.shape[0] // patches
    weight_rows = first_rows + second_rows
    part_rows = weight_rows + -(-coarse_rows // ROW_TILE) * ROW_TILE
    chips = patches // 2
    blocks = width // LANES
    far = max(groups // blocks - 1, 1)
    vmem = pl.BlockSpec(memory_space=pltpu.VMEM)

    def sems(*shape):
        return pltpu.SemaphoreType.DMA((2,) + shape)

    return pl.pallas_call(
        functools.partial(kernel, groups, patches),
        out_shape=(
            jax.ShapeDtypeStruct((edge_count, width), BF16),
            jax.ShapeDtypeStruct((node_count, width), BF16),
            jax.ShapeDtypeStruct((edge_count, width), BF16),
            jax.ShapeDtypeStruct((node_count, width), BF16),
            jax.ShapeDtypeStruct((coarse_rows, width), F32),
            jax.ShapeDtypeStruct((first_rows, width), F32),
            jax.ShapeDtypeStruct((second_rows, width), F32),
        ),
        in_specs=[pl.BlockSpec(memory_space=pltpu.SMEM)] + [vmem] * 10,
        out_specs=(vmem,) * 7,
        scratch_shapes=[
            pltpu.VMEM((patches, weight_rows, width), BF16),
            pltpu.VMEM((halo_count, width), BF16),
            pltpu.VMEM((table_rows, width), BF16),
            pltpu.VMEM((table_rows, edge_count), BF16),
            pltpu.VMEM((node_count, edge_count), BF16),
            pltpu.VMEM((edge_count, 3 * width), BF16),
        ]
        + [pltpu.VMEM((edge_count, width), BF16)] * 6
        + [
            pltpu.VMEM((halo_count, width), BF16),
            pltpu.VMEM((halo_count, width), BF16),
            pltpu.VMEM((patches, part_rows, width), BF16),
            pltpu.VMEM((chips, part_rows, width), BF16),
            pltpu.VMEM((chips, part_rows, width), BF16),
            pltpu.VMEM((blocks - 1, chips, part_rows, LANES), BF16),
            pltpu.VMEM((chips, part_rows, LANES), BF16),
            pltpu.VMEM((chips - 1, part_rows, LANES), BF16),
            pltpu.VMEM((part_rows, LANES), BF16),
            pltpu.VMEM((far, part_rows, LANES), BF16),
            pltpu.VMEM((part_rows, width), BF16),
            sems(chips - 1),
            sems(chips - 1, blocks - 1),
            sems(chips),
            sems(4),
            sems(4),
            sems(chips),
            sems(chips, blocks - 1),
            sems(chips - 1),
            sems(far),
            sems(blocks - 1),
        ],
        compiler_params=pltpu.CompilerParams(
            collective_id=0, has_side_effects=True, vmem_limit_bytes=48 * 1024 * 1024
        ),
    )(
        block_counts,
        fine_latent,
        edge_latent,
        coarse_latent,
        first_proj,
        second_proj,
        senders.reshape(1, edge_count),
        receivers.reshape(1, edge_count),
        send_rows.reshape(1, halo_count),
        cot_edges,
        cot_fine,
    )


def solution(mesh):
    both = P(("grp", "patch"), None)
    flat = P(("grp", "patch"))
    rows = P("patch", None)
    return jax.shard_map(
        functools.partial(on_device, mesh.shape["grp"], mesh.shape["patch"]),
        mesh=mesh,
        in_specs=(both, both, P(), rows, rows, flat, flat, flat, both, both, both),
        out_specs=(both, both, both, both, rows, rows, rows),
        check_vma=False,
    )
```

time: 306 us -> 68.5 us (0.22)
  waiting for transfers between devices: 200 us -> 0 us
  Pallas kernels: 0 us -> 55.1 us
  other arithmetic: 28.3 us -> 0 us
  blocking collectives: 16.9 us -> 0 us
  between operations: 14.3 us -> 0.69 us
  starting transfers between devices: 13 us -> 0 us
  matrix products: 11.6 us -> 0 us
  local copies, waits for them, and re-layouts: 21.5 us -> 12.3 us
    psum x2 -> x0, waiting for transfers between devices: 175 us -> none  [the longest x1 131 us: coarse_whole(): coarse_sum = lax.psum(coarse_part, ('grp', 'patch'))]
    pallas_call x0 -> x1, Pallas kernels: none -> 55.1 us  [on_device(): pl.pallas_call(functools.partial(kernel, groups, patches), out_shape=(jax...]
    reduce_scatter x2 -> x0, waiting for transfers between devices: 24.1 us -> none  [the longest x1 24.1 us: row_sums(): lax.psum_scatter(first_part.astype(jnp.bfloat16), 'patch', scatter_dimens...]
    all_gather x1 -> x0, blocking collectives: 16.9 us -> none  [on_device(): lax.all_gather(second_proj, 'patch', axis=0, tiled=True)]
    scatter-add x4 -> x0, other arithmetic: 13.8 us -> none  [the longest x1 4.65 us: on_device(): jax.ops.segment_sum(d_joined[:, feat_width:2 * feat_width], senders, num_...]
    ppermute x8 -> x0, starting transfers between devices: 12.7 us -> none  [shifted(): lax.ppermute(shard, axis, [(i, (i + by) % devices) for i in range(devices)])]
    dot_general x6 -> x0, matrix products: 11.6 us -> none  [the longest x1 2.86 us: on_device(): pre_act = jnp.dot(joined, first_full, preferred_element_type=jnp.float32)]
    convert_element_type x7 -> x0, other arithmetic: 8.85 us -> none  [the longest x1 2.48 us: on_device(): (cot_edges.astype(jnp.float32) + d_joined[:, :feat_width]).astype(jnp.bfl...]
  transfers between devices with their start and end apart: 13 -> 0, of which waited for: 3 -> 0; matrix products, arithmetic and copies ran while one was open for 16% -> 0% of each run, Pallas kernels for 0% -> 0%
where the time goes in v1:
time: 68.5 us; the launch traced here: 68.1 us
  Pallas kernels  55.1 us (80%)
  local copies, waits for them, and re-layouts  12.3 us (18%)
  between operations  0.69 us (1%)
    pallas_call x1, Pallas kernels, on_device(): pl.pallas_call(functools.partial(kernel, groups, patches), out_shape=(jax...  55.1 us
    unnamed x27, local copies, waits for them, and re-layouts  11.5 us

profile of v1, /device:TPU:0, one launch (start us, length us, event | category | flops | bytes accessed | tf_op | source)
XLA Modules:
  0.0 68.1 jit_solution(17180916823240827176)
XLA Ops:
  0.6 0.0 copy-start.9
  0.6 0.0 copy-start.7
  0.7 0.0 copy-start.8
  0.7 0.8 %reshape.25.list_idx_ref = s32[1,128]{1,0:T(1,128)S(1)} reshape(s32[4,32]{1,0:T(4,128)} %param.19) | data formatting | bytes 1024 | tf_op jit(solution)/shard_map/reshape | solution.py:457
  1.4 0.0 copy-done.9
  1.4 0.0 copy-done.7
  1.4 0.0 copy-done.8
  1.5 0.0 copy-start
  1.5 1.0 %copy-done = bf16[512,512]{1,0:T(8,128)(2,1)S(1)} copy-done((bf16[512,512]{1,0:T(8,128)(2,1)S(1)}, bf16[512,512]{1,0:T(8,128)(2,1)}, u32[]{:S(2)}) %copy-start) | copy-done | bytes 524312
  2.5 0.0 copy-start.1
  2.5 1.0 %copy-done.1 = bf16[512,512]{1,0:T(8,128)(2,1)S(1)} copy-done((bf16[512,512]{1,0:T(8,128)(2,1)S(1)}, bf16[512,512]{1,0:T(8,128)(2,1)}, u32[]{:S(2)}) %copy-start.1) | copy-done | bytes 524312
  3.5 0.0 copy-start.2
  3.5 0.9 %copy-done.2 = bf16[256,512]{1,0:T(8,128)(2,1)S(1)} copy-done((bf16[256,512]{1,0:T(8,128)(2,1)S(1)}, bf16[256,512]{1,0:T(8,128)(2,1)}, u32[]{:S(2)}) %copy-start.2) | copy-done | bytes 262168
  4.5 0.0 copy-start.3
  4.5 0.9 %copy-done.3 = bf16[192,512]{1,0:T(8,128)(2,1)S(1)} copy-done((bf16[192,512]{1,0:T(8,128)(2,1)S(1)}, bf16[192,512]{1,0:T(8,128)(2,1)}, u32[]{:S(2)}) %copy-start.3) | copy-done | bytes 196632
  5.4 0.0 copy-start.4
  5.4 0.9 %copy-done.4 = bf16[128,512]{1,0:T(8,128)(2,1)S(1)} copy-done((bf16[128,512]{1,0:T(8,128)(2,1)S(1)}, bf16[128,512]{1,0:T(8,128)(2,1)}, u32[]{:S(2)}) %copy-start.4) | copy-done | bytes 131096
  6.3 0.0 copy-start.5
  6.3 0.9 %copy-done.5 = bf16[128,512]{1,0:T(8,128)(2,1)S(1)} copy-done((bf16[128,512]{1,0:T(8,128)(2,1)S(1)}, bf16[128,512]{1,0:T(8,128)(2,1)}, u32[]{:S(2)}) %copy-start.5) | copy-done | bytes 131096
  7.2 0.0 copy-start.6
  7.2 0.8 %copy-done.6 = bf16[64,512]{1,0:T(8,128)(2,1)S(1)} copy-done((bf16[64,512]{1,0:T(8,128)(2,1)S(1)}, bf16[64,512]{1,0:T(8,128)(2,1)}, u32[]{:S(2)}) %copy-start.6) | copy-done | bytes 65560
  8.1 55.1 %shard_map.162 = (bf16[512,512]{1,0:T(8,128)(2,1)S(1)}, bf16[128,512]{1,0:T(8,128)(2,1)S(1)}, bf16[512,512]{1,0:T(8,128)(2,1)S(1)}, bf16[128,512]{1,0:T(8,128)(2...) custom-call(s32[4]{0:T(128)S(1)} %copy-done.9, bf16[128,512]{1,0:T(8,128)(2,1)S(1)} %copy-done.4, ...), custom_call_target="tpu_custom_call" | custom-call | tf_op jit(solution)/shard_map/pallas_call | solution.py:400
  63.1 0.8 %copy.25 = bf16[512,512]{1,0:T(8,128)(2,1)} copy(bf16[512,512]{1,0:T(8,128)(2,1)S(1)} %get-tuple-element.14) | data formatting | bytes 1048576
  63.9 0.7 copy.26
  64.6 0.8 %copy.27 = bf16[512,512]{1,0:T(8,128)(2,1)} copy(bf16[512,512]{1,0:T(8,128)(2,1)S(1)} %get-tuple-element.16) | data formatting | bytes 1048576
  65.4 0.7 copy.28
  66.0 0.6 copy.29
  66.7 0.7 %copy.30 = f32[192,512]{1,0:T(8,128)} copy(f32[192,512]{1,0:T(8,128)S(1)} %get-tuple-element.19) | data formatting | bytes 786432
  67.4 0.7 copy.31
Async XLA Ops:
  0.6 0.8 %copy-start.9 = (s32[4]{0:T(128)S(1)}, s32[4]{0:T(128)}, u32[]{:S(2)}) copy-start(s32[4]{0:T(128)} %counts_ref.1) | copy-start | bytes 52
  0.6 0.8 %copy-start.7 = (s32[512]{0:T(512)S(1)}, s32[512]{0:T(512)}, u32[]{:S(2)}) copy-start(s32[512]{0:T(512)} %param.16) | copy-start | bytes 6148
  0.7 0.8 %copy-start.8 = (s32[512]{0:T(512)S(1)}, s32[512]{0:T(512)}, u32[]{:S(2)}) copy-start(s32[512]{0:T(512)} %param.17) | copy-start | bytes 6148
  1.5 1.0 %copy-start = (bf16[512,512]{1,0:T(8,128)(2,1)S(1)}, bf16[512,512]{1,0:T(8,128)(2,1)}, u32[]{:S(2)}) copy-start(bf16[512,512]{1,0:T(8,128)(2,1)} %edge_ref.1) | copy-start | bytes 1572868
  2.5 1.0 %copy-start.1 = (bf16[512,512]{1,0:T(8,128)(2,1)S(1)}, bf16[512,512]{1,0:T(8,128)(2,1)}, u32[]{:S(2)}) copy-start(bf16[512,512]{1,0:T(8,128)(2,1)} %cot_edge_ref.1) | copy-start | bytes 1572868
  3.5 0.9 %copy-start.2 = (bf16[256,512]{1,0:T(8,128)(2,1)S(1)}, bf16[256,512]{1,0:T(8,128)(2,1)}, u32[]{:S(2)}) copy-start(bf16[256,512]{1,0:T(8,128)(2,1)} %coarse_ref.1) | copy-start | bytes 786436
  4.5 0.9 %copy-start.3 = (bf16[192,512]{1,0:T(8,128)(2,1)S(1)}, bf16[192,512]{1,0:T(8,128)(2,1)}, u32[]{:S(2)}) copy-start(bf16[192,512]{1,0:T(8,128)(2,1)} %first_ref.1) | copy-start | bytes 589828
  5.4 0.9 %copy-start.4 = (bf16[128,512]{1,0:T(8,128)(2,1)S(1)}, bf16[128,512]{1,0:T(8,128)(2,1)}, u32[]{:S(2)}) copy-start(bf16[128,512]{1,0:T(8,128)(2,1)} %fine_ref.1) | copy-start | bytes 393220
  6.3 0.9 %copy-start.5 = (bf16[128,512]{1,0:T(8,128)(2,1)S(1)}, bf16[128,512]{1,0:T(8,128)(2,1)}, u32[]{:S(2)}) copy-start(bf16[128,512]{1,0:T(8,128)(2,1)} %cot_fine_ref.1) | copy-start | bytes 393220
  7.2 0.8 %copy-start.6 = (bf16[64,512]{1,0:T(8,128)(2,1)S(1)}, bf16[64,512]{1,0:T(8,128)(2,1)}, u32[]{:S(2)}) copy-start(bf16[64,512]{1,0:T(8,128)(2,1)} %second_ref.1) | copy-start | bytes 196612

commit v2 on v1

--- a/solution.py
+++ b/solution.py
@@ -40,12 +40,23 @@
 def kernel(
     groups,
     patches,
+    counts_hbm,
+    fine_hbm,
+    edge_hbm,
+    coarse_hbm,
+    first_hbm,
+    second_hbm,
+    send_idx_hbm,
+    recv_idx_hbm,
+    list_idx_hbm,
+    cot_edge_hbm,
+    cot_fine_hbm,
+    new_edges_hbm,
+    fine_msg_hbm,
+    grad_edges_hbm,
+    grad_fine_hbm,
+    result,
     counts_ref,
-    fine_ref,
-    edge_ref,
-    coarse_ref,
-    first_ref,
-    second_ref,
     send_idx_ref,
     recv_idx_ref,
     list_idx_ref,
@@ -55,9 +66,6 @@
     fine_msg_ref,
     grad_edges_ref,
     grad_fine_ref,
-    grad_coarse_ref,
-    grad_first_ref,
-    grad_second_ref,
     weights,
     outgoing,
     table,
@@ -80,7 +88,8 @@
     from_z,
     whole_sum,
     from_far,
-    result,
+    in_sems,
+    out_sems,
     w_z_sems,
     w_grp_sems,
     w_core_sems,
@@ -97,18 +106,18 @@
     z = b // 2
     c = b % 2
     chips = patches // 2
-    width = fine_ref.shape[1]
+    width = fine_hbm.shape[1]
     blocks = width // LANES
     k = a % blocks
     base = a - k
     far_count = groups // blocks
-    first_rows = first_ref.shape[0]
-    second_rows = second_ref.shape[0]
-    coarse_rows = grad_coarse_ref.shape[0]
-    node_count = fine_ref.shape[0]
-    halo_count = list_idx_ref.shape[1]
-    list_rows = halo_count // 4
-    edge_count = edge_ref.shape[0]
+    first_rows = first_hbm.shape[0]
+    second_rows = second_hbm.shape[0]
+    coarse_rows = coarse_hbm.shape[0] // patches
+    node_count = fine_hbm.shape[0]
+    list_rows = list_idx_hbm.shape[1]
+    halo_count = 4 * list_rows
+    edge_count = edge_hbm.shape[0]
     weight_rows = first_rows + second_rows
     part_rows = parts.shape[1]
     sibling = (a, 2 * z + 1 - c)
@@ -163,10 +172,35 @@
         pl.semaphore_signal(
             barrier, inc=1, device_id=((a + step) % groups, b), device_id_type=pl.DeviceIdType.MESH
         )
-    weights[b, :first_rows, :] = first_ref[...]
-    weights[b, first_rows:, :] = second_ref[...]
-    pick_list = picks(node_count, list_idx_ref[...])
-    outgoing[...] = dot_tn(pick_list, fine_ref[...]).astype(BF16)
+    fine_ref = table.at[:node_count, :]
+    incoming = [
+        pltpu.make_async_copy(src, dst, in_sems.at[at])
+        for at, (src, dst) in enumerate(
+            (
+                (first_hbm, weights.at[b, :first_rows, :]),
+                (second_hbm, weights.at[b, first_rows:, :]),
+                (list_idx_hbm, list_idx_ref),
+                (fine_hbm, fine_ref),
+                (recv_idx_hbm, recv_idx_ref),
+                (send_idx_hbm, send_idx_ref),
+                (edge_hbm, joined.at[:, :width]),
+                (coarse_hbm, table.at[node_count + halo_count :, :]),
+                (counts_hbm, counts_ref),
+                (cot_edge_hbm, cot_edge_ref),
+                (cot_fine_hbm, cot_fine_ref),
+            )
+        )
+    ]
+    for copy in incoming:
+        copy.start()
+    for copy in incoming[2:4]:
+        copy.wait()
+    for own in range(4):
+        outgoing[own * list_rows : (own + 1) * list_rows, :] = dot_tn(
+            picks(node_count, list_idx_ref[own : own + 1, :]), fine_ref[...]
+        ).astype(BF16)
+    for copy in incoming[:2]:
+        copy.wait()
     pl.semaphore_wait(barrier, patches + groups - 2)
 
     along_z = [
@@ -181,8 +215,8 @@
     ]
     between = [send(weights.at[b], weights.at[b], w_core_sems, (0,), sibling)]
     halo = exchange(outgoing, table, node_count, halo_sems)
-    table[:node_count, :] = fine_ref[...]
-    table[node_count + halo_count :, :] = coarse_ref[...]
+    for copy in incoming[4:]:
+        copy.wait()
     over_grp = []
     for step in range(1, chips):
         along_z[step - 1].wait_recv()
@@ -201,7 +235,6 @@
         )
     pick_send[...] = picks(table.shape[0], send_idx_ref[...])
     pick_recv[...] = picks(node_count, recv_idx_ref[...])
-    joined[:, :width] = edge_ref[...]
     joined[:, 2 * width :] = dot_tn(pick_recv[...], fine_ref[...]).astype(BF16)
     for step in range(1, chips):
         for copy in over_grp[step - 1]:
@@ -239,7 +272,7 @@
         live = (position < bound).astype(F32)
         message = live * normed
         message_all[rows, :] = message.astype(BF16)
-        new_edges_ref[rows, :] = (edge_ref[rows, :].astype(F32) + message).astype(BF16)
+        new_edges_ref[rows, :] = (joined[rows, :width].astype(F32) + message).astype(BF16)
         cot = cot_edge_ref[rows, :].astype(F32)
         upstream = live * (cot + dot_tn(pick_recv[:, rows], cot_fine_ref[...]))
         d_outer = (
@@ -252,6 +285,13 @@
         grad_edges_ref[rows, :] = (cot + dot_nt(d_pre, first_full[:width])).astype(BF16)
         d_send_all[rows, :] = dot_nt(d_pre, first_full[width : 2 * width]).astype(BF16)
         d_recv_all[rows, :] = dot_nt(d_pre, first_full[2 * width :]).astype(BF16)
+
+    leaving = [
+        pltpu.make_async_copy(new_edges_ref, new_edges_hbm, out_sems.at[0]),
+        pltpu.make_async_copy(grad_edges_ref, grad_edges_hbm, out_sems.at[1]),
+    ]
+    for copy in leaving:
+        copy.start()
 
     halo_back[...] = dot(
         pick_send[node_count : node_count + halo_count, :], d_send_all[...]
@@ -276,16 +316,17 @@
             parts[at * held + place, :first_rows, :] = part[
                 place * first_rows : (place + 1) * first_rows
             ]
-        for chip in range(at * held // 2, (at + 1) * held // 2):
-            to_core.append(
-                send(
-                    parts.at[2 * chip + 1 - c], from_core.at[chip], core_sems, (chip,), sibling
-                )
-            )
-
+    for turn in range(chips):
+        chip = chip_at(turn)
+        to_core.append(
+            send(parts.at[2 * chip + 1 - c], from_core.at[chip], core_sems, (turn,), sibling)
+        )
+
+    turns = list(range(1, chips)) + [0]
     to_grp = []
-    for chip in range(chips):
-        to_core[chip].wait_recv()
+    for turn in turns:
+        chip = chip_at(turn)
+        to_core[turn].wait_recv()
         chip_sum[chip] = (parts[2 * chip + c].astype(F32) + from_core[chip].astype(F32)).astype(
             BF16
         )
@@ -293,40 +334,50 @@
             [
                 send(
                     chip_sum.at[chip, :, columns((k + offset) % blocks)],
-                    from_grp.at[offset - 1, chip],
+                    from_grp.at[offset - 1, turn],
                     grp_sems,
-                    (chip, offset - 1),
+                    (turn, offset - 1),
                     peer(offset),
                 )
                 for offset in range(1, blocks)
             ]
         )
+    to_z = []
+    for turn in turns:
+        chip = chip_at(turn)
+        total = chip_sum[chip, :, columns(k)].astype(F32)
+        for offset in range(1, blocks):
+            to_grp[turn - 1][offset - 1].wait_recv()
+            total = total + from_grp[offset - 1, turn].astype(F32)
+        if turn:
+            plane_sum[turn - 1] = total.astype(BF16)
+            to_z.append(
+                send(
+                    plane_sum.at[turn - 1],
+                    from_z.at[turn - 1],
+                    z_sems,
+                    (turn - 1,),
+                    (a, 2 * chip + c),
+                )
+            )
     fine_msg_ref[...] = dot(pick_recv[...], message_all[...]).astype(BF16)
     local_grad = dot(pick_send[:node_count, :], d_send_all[...]) + dot(
         pick_recv[...], d_recv_all[...]
     )
-    for copy in back:
-        copy.wait_recv()
-    grad_fine_ref[...] = (
-        local_grad + dot(picks(node_count, list_idx_ref[...]), returned[...])
-    ).astype(BF16)
-    for chip in range(chips):
-        total = chip_sum[chip, :, columns(k)].astype(F32)
-        for offset in range(1, blocks):
-            to_grp[chip][offset - 1].wait_recv()
-            total = total + from_grp[offset - 1, chip].astype(F32)
-        plane_sum[chip] = total.astype(BF16)
-    to_z = [
-        send(
-            plane_sum.at[chip_at(step)],
-            from_z.at[step - 1],
-            z_sems,
-            (step - 1,),
-            (a, 2 * chip_at(step) + c),
-        )
-        for step in range(1, chips)
+    for own in range(4):
+        back[own].wait_recv()
+    for own in range(4):
+        local_grad = local_grad + dot(
+            picks(node_count, list_idx_ref[own : own + 1, :]),
+            returned[own * list_rows : (own + 1) * list_rows, :],
+        )
+    grad_fine_ref[...] = local_grad.astype(BF16)
+    leaving += [
+        pltpu.make_async_copy(fine_msg_ref, fine_msg_hbm, out_sems.at[2]),
+        pltpu.make_async_copy(grad_fine_ref, grad_fine_hbm, out_sems.at[3]),
     ]
-    total = plane_sum[z].astype(F32)
+    for copy in leaving[2:]:
+        copy.start()
     for step in range(1, chips):
         to_z[step - 1].wait_recv()
         total = total + from_z[step - 1].astype(F32)
@@ -358,11 +409,26 @@
     ]
     for copy in shares:
         copy.wait_recv()
-    grad_first_ref[...] = result[:first_rows, :].astype(F32)
-    grad_second_ref[...] = result[first_rows:weight_rows, :].astype(F32)
-    grad_coarse_ref[...] = result[weight_rows:, :].astype(F32)[:coarse_rows]
+    for copy in leaving:
+        copy.wait()
     for copy in pending:
         copy.wait_send()
+
+
+def finish(first_rows, second_rows, result, *refs):
+    sources, targets, shares, sems = refs[:4], refs[4:8], refs[8:11], refs[11]
+    copies = [
+        pltpu.make_async_copy(source, target, sems.at[at])
+        for at, (source, target) in enumerate(zip(sources, targets))
+    ]
+    for copy in copies:
+        copy.start()
+    weight_rows = first_rows + second_rows
+    shares[0][...] = result[weight_rows:, :].astype(F32)[: shares[0].shape[0]]
+    shares[1][...] = result[:first_rows, :].astype(F32)
+    shares[2][...] = result[first_rows:weight_rows, :].astype(F32)
+    for copy in copies:
+        copy.wait()
 
 
 def on_device(
@@ -393,24 +459,33 @@
     blocks = width // LANES
     far = max(groups // blocks - 1, 1)
     vmem = pl.BlockSpec(memory_space=pltpu.VMEM)
+    hbm = pl.BlockSpec(memory_space=pltpu.HBM)
 
     def sems(*shape):
         return pltpu.SemaphoreType.DMA((2,) + shape)
 
-    return pl.pallas_call(
+    rows_out = (
+        jax.ShapeDtypeStruct((edge_count, width), BF16),
+        jax.ShapeDtypeStruct((node_count, width), BF16),
+        jax.ShapeDtypeStruct((edge_count, width), BF16),
+        jax.ShapeDtypeStruct((node_count, width), BF16),
+    )
+    *rows, result = pl.pallas_call(
         functools.partial(kernel, groups, patches),
-        out_shape=(
-            jax.ShapeDtypeStruct((edge_count, width), BF16),
-            jax.ShapeDtypeStruct((node_count, width), BF16),
-            jax.ShapeDtypeStruct((edge_count, width), BF16),
-            jax.ShapeDtypeStruct((node_count, width), BF16),
-            jax.ShapeDtypeStruct((coarse_rows, width), F32),
-            jax.ShapeDtypeStruct((first_rows, width), F32),
-            jax.ShapeDtypeStruct((second_rows, width), F32),
-        ),
-        in_specs=[pl.BlockSpec(memory_space=pltpu.SMEM)] + [vmem] * 10,
-        out_specs=(vmem,) * 7,
+        out_shape=rows_out + (jax.ShapeDtypeStruct((part_rows, width), BF16),),
+        in_specs=[hbm] * 11,
+        out_specs=(hbm,) * 4 + (vmem,),
         scratch_shapes=[
+            pltpu.SMEM(block_counts.shape, jnp.int32),
+            pltpu.VMEM((1, edge_count), jnp.int32),
+            pltpu.VMEM((1, edge_count), jnp.int32),
+            pltpu.VMEM(send_rows.shape, jnp.int32),
+            pltpu.VMEM((edge_count, width), BF16),
+            pltpu.VMEM((node_count, width), BF16),
+            pltpu.VMEM((edge_count, width), BF16),
+            pltpu.VMEM((node_count, width), BF16),
+            pltpu.VMEM((edge_count, width), BF16),
+            pltpu.VMEM((node_count, width), BF16),
             pltpu.VMEM((patches, weight_rows, width), BF16),
             pltpu.VMEM((halo_count, width), BF16),
             pltpu.VMEM((table_rows, width), BF16),
@@ -426,11 +501,12 @@
             pltpu.VMEM((chips, part_rows, width), BF16),
             pltpu.VMEM((chips, part_rows, width), BF16),
             pltpu.VMEM((blocks - 1, chips, part_rows, LANES), BF16),
-            pltpu.VMEM((chips, part_rows, LANES), BF16),
+            pltpu.VMEM((chips - 1, part_rows, LANES), BF16),
             pltpu.VMEM((chips - 1, part_rows, LANES), BF16),
             pltpu.VMEM((part_rows, LANES), BF16),
             pltpu.VMEM((far, part_rows, LANES), BF16),
-            pltpu.VMEM((part_rows, width), BF16),
+            pltpu.SemaphoreType.DMA((11,)),
+            pltpu.SemaphoreType.DMA((4,)),
             sems(chips - 1),
             sems(chips - 1, blocks - 1),
             sems(chips),
@@ -443,7 +519,7 @@
             sems(blocks - 1),
         ],
         compiler_params=pltpu.CompilerParams(
-            collective_id=0, has_side_effects=True, vmem_limit_bytes=48 * 1024 * 1024
+            collective_id=0, has_side_effects=True, vmem_limit_bytes=62 * 1024 * 1024
         ),
     )(
         block_counts,
@@ -454,10 +530,21 @@
         second_proj,
         senders.reshape(1, edge_count),
         receivers.reshape(1, edge_count),
-        send_rows.reshape(1, halo_count),
+        send_rows,
         cot_edges,
         cot_fine,
     )
+    shares = tuple(
+        jax.ShapeDtypeStruct((count, width), F32)
+        for count in (coarse_rows, first_rows, second_rows)
+    )
+    return pl.pallas_call(
+        functools.partial(finish, first_rows, second_rows),
+        out_shape=rows_out + shares,
+        in_specs=[vmem] * 5,
+        out_specs=(hbm,) * 4 + (vmem,) * 3,
+        scratch_shapes=[pltpu.SemaphoreType.DMA((4,))],
+    )(result, *rows)
 
 
 def solution(mesh):

time: 68.5 us -> 54.1 us (0.79)
  local copies, waits for them, and re-layouts: 12.3 us -> 0 us
  Pallas kernels: 55.1 us -> 53.3 us
    unnamed x27 -> x0, local copies, waits for them, and re-layouts: 11.5 us -> none
    pallas_call x1 -> x2, Pallas kernels: 55.1 us -> 53.3 us  [the longest x1 50 us: on_device(): pl.pallas_call(functools.partial(kernel, groups, patches), out_shape=rows...]
    reshape x1 -> x0, local copies, waits for them, and re-layouts: 0.78 us -> none  [on_device(): send_rows.reshape(1, halo_count)]
where the time goes in v2:
time: 54.1 us; the launch traced here: 53.9 us
  Pallas kernels  53.3 us (99%)
  between operations  0.64 us (1%)
    pallas_call x1, Pallas kernels, on_device(): pl.pallas_call(functools.partial(kernel, groups, patches), out_shape=rows...  50 us
    pallas_call x1, Pallas kernels, on_device(): pl.pallas_call(functools.partial(finish, first_rows, second_rows), out_sh...  3.23 us

profile of v2, /device:TPU:0, one launch (start us, length us, event | category | flops | bytes accessed | tf_op | source)
XLA Modules:
  0.0 53.9 jit_solution(14877842532903425686)
XLA Ops:
  0.6 50.0 %shard_map.162 = (bf16[512,512]{1,0:T(8,128)(2,1)}, bf16[128,512]{1,0:T(8,128)(2,1)}, bf16[512,512]{1,0:T(8,128)(2,1)}, bf16[128,512]{1,0:T(8,128)(2,1)}, bf16[288,512]{1,0:T(8,128)(2,1)}) custom-call(s32[4]{0:T(128)} %counts_hbm.1, bf16[128,512]{1,0:T(8,128)(2,1)} %fine_hbm.1, bf16[512,512]{1,0:T(8,128)(2,1)} %edge_hbm.1, bf16[256,512]{1,0:T(8,128)(2,1)} %coarse_hbm.1, ...), custom_call_target="tpu_custom_call" | custom-call | tf_op jit(solution)/shard_map/pallas_call | solution.py:473
  50.7 3.2 %shard_map.163 = (bf16[512,512]{1,0:T(8,128)(2,1)}, bf16[128,512]{1,0:T(8,128)(2,1)}, bf16[512,512]{1,0:T(8,128)(2,1)}, bf16[128,512]{1,0:T(8,128)(2,1)}, f32[32...) custom-call(bf16[288,512]{1,0:T(8,128)(2,1)} %get-tuple-element.12.result, ...), custom_call_target="tpu_custom_call" | custom-call | tf_op jit(solution)/shard_map/pallas_call | solution.py:541

commit v3 on v2

--- a/solution.py
+++ b/solution.py
@@ -76,6 +76,7 @@
     d_outer_all,
     d_pre_all,
     message_all,
+    upstream_all,
     d_send_all,
     d_recv_all,
     halo_back,
@@ -83,7 +84,9 @@
     parts,
     from_core,
     chip_sum,
-    from_grp,
+    from_one,
+    pair_sum,
+    from_two,
     plane_sum,
     from_z,
     whole_sum,
@@ -193,51 +196,56 @@
     ]
     for copy in incoming:
         copy.start()
+    for copy in incoming[:2]:
+        copy.wait()
+    pl.semaphore_wait(barrier, patches + groups - 2)
+
+    order = [step for near in range(1, chips) for step in (near, chips - near)][: chips - 1]
+    along_z = {}
+
+    def start_z(step):
+        along_z[step] = send(
+            weights.at[b, :, columns(k)],
+            weights.at[b, :, columns(k)],
+            w_z_sems,
+            (step - 1,),
+            (a, 2 * chip_at(step) + c),
+        )
+
+    for step in order[:2]:
+        start_z(step)
+    between = [send(weights.at[b], weights.at[b], w_core_sems, (0,), sibling)]
     for copy in incoming[2:4]:
         copy.wait()
     for own in range(4):
         outgoing[own * list_rows : (own + 1) * list_rows, :] = dot_tn(
             picks(node_count, list_idx_ref[own : own + 1, :]), fine_ref[...]
         ).astype(BF16)
-    for copy in incoming[:2]:
-        copy.wait()
-    pl.semaphore_wait(barrier, patches + groups - 2)
-
-    along_z = [
-        send(
-            weights.at[b, :, columns(k)],
-            weights.at[b, :, columns(k)],
-            w_z_sems,
-            (step - 1,),
-            (a, 2 * chip_at(step) + c),
-        )
-        for step in range(1, chips)
-    ]
-    between = [send(weights.at[b], weights.at[b], w_core_sems, (0,), sibling)]
     halo = exchange(outgoing, table, node_count, halo_sems)
     for copy in incoming[4:]:
         copy.wait()
-    over_grp = []
-    for step in range(1, chips):
-        along_z[step - 1].wait_recv()
+    over_grp = {}
+    for at, step in enumerate(order):
+        along_z[step].wait_recv()
+        for later in order[at + 2 : at + 3]:
+            start_z(later)
         owner = 2 * chip_at(-step) + c
-        over_grp.append(
-            [
-                send(
-                    weights.at[owner, :, columns(k)],
-                    weights.at[owner, :, columns(k)],
-                    w_grp_sems,
-                    (step - 1, offset - 1),
-                    peer(offset),
-                )
-                for offset in range(1, blocks)
-            ]
-        )
+        over_grp[step] = [
+            send(
+                weights.at[owner, :, columns(k)],
+                weights.at[owner, :, columns(k)],
+                w_grp_sems,
+                (step - 1, offset - 1),
+                peer(offset),
+            )
+            for offset in range(1, blocks)
+        ]
     pick_send[...] = picks(table.shape[0], send_idx_ref[...])
     pick_recv[...] = picks(node_count, recv_idx_ref[...])
     joined[:, 2 * width :] = dot_tn(pick_recv[...], fine_ref[...]).astype(BF16)
-    for step in range(1, chips):
-        for copy in over_grp[step - 1]:
+    upstream_all[...] = cot_edge_ref[...].astype(F32) + dot_tn(pick_recv[...], cot_fine_ref[...])
+    for step in order:
+        for copy in over_grp[step]:
             copy.wait_recv()
         owner = 2 * chip_at(-step) + c
         between.append(
@@ -271,10 +279,8 @@
             )
         live = (position < bound).astype(F32)
         message = live * normed
-        message_all[rows, :] = message.astype(BF16)
-        new_edges_ref[rows, :] = (joined[rows, :width].astype(F32) + message).astype(BF16)
-        cot = cot_edge_ref[rows, :].astype(F32)
-        upstream = live * (cot + dot_tn(pick_recv[:, rows], cot_fine_ref[...]))
+        message_all[rows, :] = message
+        upstream = live * upstream_all[rows, :]
         d_outer = (
             (upstream - row_mean(upstream) - normed * row_mean(upstream * normed)) * inv_scale
         ).astype(BF16)
@@ -282,16 +288,7 @@
         d_hidden = dot_nt(d_outer, second_full)
         d_pre = (d_hidden * gate_sig * (1.0 + pre_act * (1.0 - gate_sig))).astype(BF16)
         d_pre_all[rows, :] = d_pre
-        grad_edges_ref[rows, :] = (cot + dot_nt(d_pre, first_full[:width])).astype(BF16)
         d_send_all[rows, :] = dot_nt(d_pre, first_full[width : 2 * width]).astype(BF16)
-        d_recv_all[rows, :] = dot_nt(d_pre, first_full[2 * width :]).astype(BF16)
-
-    leaving = [
-        pltpu.make_async_copy(new_edges_ref, new_edges_hbm, out_sems.at[0]),
-        pltpu.make_async_copy(grad_edges_ref, grad_edges_hbm, out_sems.at[1]),
-    ]
-    for copy in leaving:
-        copy.start()
 
     halo_back[...] = dot(
         pick_send[node_count : node_count + halo_count, :], d_send_all[...]
@@ -306,49 +303,58 @@
             own_coarse = jnp.concatenate([own_coarse, jnp.zeros((spare, width), BF16)], axis=0)
         parts[at, first_rows:weight_rows, :] = second_part[at * second_rows : (at + 1) * second_rows]
         parts[at, weight_rows:, :] = own_coarse
-    to_core = []
-    held = PART_ROWS // first_rows
-    for at in range(patches // held):
-        part = dot_tn(
-            joined[:, at * PART_ROWS : (at + 1) * PART_ROWS], d_pre_all[...]
-        ).astype(BF16)
-        for place in range(held):
-            parts[at * held + place, :first_rows, :] = part[
-                place * first_rows : (place + 1) * first_rows
-            ]
-    for turn in range(chips):
+    turns = list(range(1, chips)) + [0]
+    k_hi, k_lo = k // 2, k % 2
+    across_lo = (base + 2 * k_hi + 1 - k_lo, b)
+    across_hi = (base + 2 * (1 - k_hi) + k_lo, b)
+    to_core, to_one, to_two, to_z = {}, {}, {}, []
+    pair_rows = 2 * first_rows
+    by_chip = pair_rows % LANES == 0
+
+    def form(turn):
         chip = chip_at(turn)
-        to_core.append(
-            send(parts.at[2 * chip + 1 - c], from_core.at[chip], core_sems, (turn,), sibling)
-        )
-
-    turns = list(range(1, chips)) + [0]
-    to_grp = []
-    for turn in turns:
+        if by_chip:
+            span = pl.ds(pl.multiple_of(chip * pair_rows, LANES), pair_rows)
+            part = dot_tn(joined[:, span], d_pre_all[...]).astype(BF16)
+            parts[2 * chip, :first_rows, :] = part[:first_rows]
+            parts[2 * chip + 1, :first_rows, :] = part[first_rows:]
+        to_core[turn] = send(
+            parts.at[2 * chip + 1 - c], from_core.at[turn], core_sems, (turn,), sibling
+        )
+
+    def sum_cores(turn):
         chip = chip_at(turn)
         to_core[turn].wait_recv()
-        chip_sum[chip] = (parts[2 * chip + c].astype(F32) + from_core[chip].astype(F32)).astype(
-            BF16
-        )
-        to_grp.append(
-            [
-                send(
-                    chip_sum.at[chip, :, columns((k + offset) % blocks)],
-                    from_grp.at[offset - 1, turn],
-                    grp_sems,
-                    (turn, offset - 1),
-                    peer(offset),
-                )
-                for offset in range(1, blocks)
-            ]
-        )
-    to_z = []
-    for turn in turns:
+        for hi in range(2):
+            for lo in range(2):
+                block = 2 * hi + lo
+                span = slice(block * LANES, (block + 1) * LANES)
+                chip_sum[turn, hi, lo] = (
+                    parts[2 * chip + c, :, span].astype(F32) + from_core[turn, :, span].astype(F32)
+                ).astype(BF16)
+        if turn % 2:
+            source, device = chip_sum.at[turn, :, 1 - k_lo], across_lo
+        else:
+            source, device = chip_sum.at[turn, 1 - k_hi], across_hi
+        to_one[turn] = send(source, from_one.at[turn], grp_sems, (turn, 0), device)
+
+    def sum_pair(turn):
+        to_one[turn].wait_recv()
+        for half in range(2):
+            own = chip_sum[turn, half, k_lo] if turn % 2 else chip_sum[turn, k_hi, half]
+            pair_sum[turn, half] = (own.astype(F32) + from_one[turn, half].astype(F32)).astype(
+                BF16
+            )
+        other, device = (1 - k_hi, across_hi) if turn % 2 else (1 - k_lo, across_lo)
+        to_two[turn] = send(
+            pair_sum.at[turn, other], from_two.at[turn], grp_sems, (turn, 1), device
+        )
+
+    def sum_plane(turn):
         chip = chip_at(turn)
-        total = chip_sum[chip, :, columns(k)].astype(F32)
-        for offset in range(1, blocks):
-            to_grp[turn - 1][offset - 1].wait_recv()
-            total = total + from_grp[offset - 1, turn].astype(F32)
+        to_two[turn].wait_recv()
+        own = pair_sum[turn, k_hi if turn % 2 else k_lo]
+        total = own.astype(F32) + from_two[turn].astype(F32)
         if turn:
             plane_sum[turn - 1] = total.astype(BF16)
             to_z.append(
@@ -360,24 +366,60 @@
                     (a, 2 * chip + c),
                 )
             )
-    fine_msg_ref[...] = dot(pick_recv[...], message_all[...]).astype(BF16)
-    local_grad = dot(pick_send[:node_count, :], d_send_all[...]) + dot(
-        pick_recv[...], d_recv_all[...]
-    )
-    for own in range(4):
-        back[own].wait_recv()
-    for own in range(4):
-        local_grad = local_grad + dot(
-            picks(node_count, list_idx_ref[own : own + 1, :]),
-            returned[own * list_rows : (own + 1) * list_rows, :],
-        )
-    grad_fine_ref[...] = local_grad.astype(BF16)
-    leaving += [
-        pltpu.make_async_copy(fine_msg_ref, fine_msg_hbm, out_sems.at[2]),
-        pltpu.make_async_copy(grad_fine_ref, grad_fine_hbm, out_sems.at[3]),
-    ]
-    for copy in leaving[2:]:
+        return total
+
+    if not by_chip:
+        held = PART_ROWS // first_rows
+        for at in range(patches // held):
+            part = dot_tn(
+                joined[:, at * PART_ROWS : (at + 1) * PART_ROWS], d_pre_all[...]
+            ).astype(BF16)
+            for place in range(held):
+                parts[at * held + place, :first_rows, :] = part[
+                    place * first_rows : (place + 1) * first_rows
+                ]
+    def finish_edges():
+        new_edges_ref[...] = (joined[:, :width].astype(F32) + message_all[...]).astype(BF16)
+        first_full = weights[:, :first_rows, :].reshape(patches * first_rows, width)
+        grad_edges_ref[...] = (
+            cot_edge_ref[...].astype(F32) + dot_nt(d_pre_all[...], first_full[:width])
+        ).astype(BF16)
+        d_recv_all[...] = dot_nt(d_pre_all[...], first_full[2 * width :]).astype(BF16)
+        leave(new_edges_ref, new_edges_hbm, 0)
+        leave(grad_edges_ref, grad_edges_hbm, 1)
+
+    def finish_nodes():
+        fine_msg_ref[...] = dot(pick_recv[...], message_all[...].astype(BF16)).astype(BF16)
+        local_grad = dot(pick_send[:node_count, :], d_send_all[...]) + dot(
+            pick_recv[...], d_recv_all[...]
+        )
+        for own in range(4):
+            back[own].wait_recv()
+        for own in range(4):
+            local_grad = local_grad + dot(
+                picks(node_count, list_idx_ref[own : own + 1, :]),
+                returned[own * list_rows : (own + 1) * list_rows, :],
+            )
+        grad_fine_ref[...] = local_grad.astype(BF16)
+        leave(fine_msg_ref, fine_msg_hbm, 2)
+        leave(grad_fine_ref, grad_fine_hbm, 3)
+
+    leaving = []
+
+    def leave(source, target, at):
+        copy = pltpu.make_async_copy(source, target, out_sems.at[at])
         copy.start()
+        leaving.append(copy)
+
+    stages = (form, sum_cores, sum_pair, sum_plane)
+    for at in range(chips + len(stages) - 1):
+        for delay, stage in enumerate(stages):
+            if 0 <= at - delay < chips:
+                total = stage(turns[at - delay])
+        if at == chips:
+            finish_edges()
+        if at == chips + 1:
+            finish_nodes()
     for step in range(1, chips):
         to_z[step - 1].wait_recv()
         total = total + from_z[step - 1].astype(F32)
@@ -493,14 +535,18 @@
             pltpu.VMEM((node_count, edge_count), BF16),
             pltpu.VMEM((edge_count, 3 * width), BF16),
         ]
-        + [pltpu.VMEM((edge_count, width), BF16)] * 6
+        + [pltpu.VMEM((edge_count, width), BF16)] * 3
+        + [pltpu.VMEM((edge_count, width), F32)] * 2
+        + [pltpu.VMEM((edge_count, width), BF16)] * 2
         + [
             pltpu.VMEM((halo_count, width), BF16),
             pltpu.VMEM((halo_count, width), BF16),
             pltpu.VMEM((patches, part_rows, width), BF16),
             pltpu.VMEM((chips, part_rows, width), BF16),
-            pltpu.VMEM((chips, part_rows, width), BF16),
-            pltpu.VMEM((blocks - 1, chips, part_rows, LANES), BF16),
+            pltpu.VMEM((chips, 2, 2, part_rows, LANES), BF16),
+            pltpu.VMEM((chips, 2, part_rows, LANES), BF16),
+            pltpu.VMEM((chips, 2, part_rows, LANES), BF16),
+            pltpu.VMEM((chips, part_rows, LANES), BF16),
             pltpu.VMEM((chips - 1, part_rows, LANES), BF16),
             pltpu.VMEM((chips - 1, part_rows, LANES), BF16),
             pltpu.VMEM((part_rows, LANES), BF16),
@@ -513,7 +559,7 @@
             sems(4),
             sems(4),
             sems(chips),
-            sems(chips, blocks - 1),
+            sems(chips, 2),
             sems(chips - 1),
             sems(far),
             sems(blocks - 1),

time: 54.1 us -> 53.1 us (0.982)
  Pallas kernels: 53.3 us -> 52.3 us
    pallas_call x1, Pallas kernels: 50 us -> 49.1 us  [on_device(): pl.pallas_call(functools.partial(kernel, groups, patches), out_shape=rows...]
where the time goes in v3:
time: 53.1 us; the launch traced here: 53 us
  Pallas kernels  52.3 us (98%)
  between operations  0.64 us (1%)
    pallas_call x1, Pallas kernels, on_device(): pl.pallas_call(functools.partial(kernel, groups, patches), out_shape=rows...  49.1 us
    pallas_call x1, Pallas kernels, on_device(): pl.pallas_call(functools.partial(finish, first_rows, second_rows), out_sh...  3.23 us

profile of v3, /device:TPU:0, one launch (start us, length us, event | category | flops | bytes accessed | tf_op | source)
XLA Modules:
  0.0 53.0 jit_solution(4321916560007449644)
XLA Ops:
  0.6 49.1 %shard_map.162 = (bf16[512,512]{1,0:T(8,128)(2,1)}, bf16[128,512]{1,0:T(8,128)(2,1)}, bf16[512,512]{1,0:T(8,128)(2,1)}, bf16[128,512]{1,0:T(8,128)(2,1)}, bf16[288,512]{1,0:T(8,128)(2,1)}) custom-call(s32[4]{0:T(128)} %counts_hbm.1, bf16[128,512]{1,0:T(8,128)(2,1)} %fine_hbm.1, bf16[512,512]{1,0:T(8,128)(2,1)} %edge_hbm.1, bf16[256,512]{1,0:T(8,128)(2,1)} %coarse_hbm.1, ...), custom_call_target="tpu_custom_call" | custom-call | tf_op jit(solution)/shard_map/pallas_call | solution.py:515
  49.7 3.2 %shard_map.163 = (bf16[512,512]{1,0:T(8,128)(2,1)}, bf16[128,512]{1,0:T(8,128)(2,1)}, bf16[512,512]{1,0:T(8,128)(2,1)}, bf16[128,512]{1,0:T(8,128)(2,1)}, f32[32...) custom-call(bf16[288,512]{1,0:T(8,128)(2,1)} %get-tuple-element.12.result, ...), custom_call_target="tpu_custom_call" | custom-call | tf_op jit(solution)/shard_map/pallas_call | solution.py:587

commit v4 on v3

--- a/solution.py
+++ b/solution.py
@@ -84,9 +84,7 @@
     parts,
     from_core,
     chip_sum,
-    from_one,
-    pair_sum,
-    from_two,
+    from_grp,
     plane_sum,
     from_z,
     whole_sum,
@@ -304,10 +302,7 @@
         parts[at, first_rows:weight_rows, :] = second_part[at * second_rows : (at + 1) * second_rows]
         parts[at, weight_rows:, :] = own_coarse
     turns = list(range(1, chips)) + [0]
-    k_hi, k_lo = k // 2, k % 2
-    across_lo = (base + 2 * k_hi + 1 - k_lo, b)
-    across_hi = (base + 2 * (1 - k_hi) + k_lo, b)
-    to_core, to_one, to_two, to_z = {}, {}, {}, []
+    to_core, to_grp, to_z = {}, {}, []
     pair_rows = 2 * first_rows
     by_chip = pair_rows % LANES == 0
 
@@ -325,36 +320,28 @@
     def sum_cores(turn):
         chip = chip_at(turn)
         to_core[turn].wait_recv()
-        for hi in range(2):
-            for lo in range(2):
-                block = 2 * hi + lo
-                span = slice(block * LANES, (block + 1) * LANES)
-                chip_sum[turn, hi, lo] = (
-                    parts[2 * chip + c, :, span].astype(F32) + from_core[turn, :, span].astype(F32)
-                ).astype(BF16)
-        if turn % 2:
-            source, device = chip_sum.at[turn, :, 1 - k_lo], across_lo
-        else:
-            source, device = chip_sum.at[turn, 1 - k_hi], across_hi
-        to_one[turn] = send(source, from_one.at[turn], grp_sems, (turn, 0), device)
-
-    def sum_pair(turn):
-        to_one[turn].wait_recv()
-        for half in range(2):
-            own = chip_sum[turn, half, k_lo] if turn % 2 else chip_sum[turn, k_hi, half]
-            pair_sum[turn, half] = (own.astype(F32) + from_one[turn, half].astype(F32)).astype(
-                BF16
-            )
-        other, device = (1 - k_hi, across_hi) if turn % 2 else (1 - k_lo, across_lo)
-        to_two[turn] = send(
-            pair_sum.at[turn, other], from_two.at[turn], grp_sems, (turn, 1), device
-        )
+        for block in range(blocks):
+            span = slice(block * LANES, (block + 1) * LANES)
+            chip_sum[turn, block] = (
+                parts[2 * chip + c, :, span].astype(F32) + from_core[turn, :, span].astype(F32)
+            ).astype(BF16)
+        to_grp[turn] = [
+            send(
+                chip_sum.at[turn, (k + offset) % blocks],
+                from_grp.at[offset - 1, turn],
+                grp_sems,
+                (turn, offset - 1),
+                peer(offset),
+            )
+            for offset in range(1, blocks)
+        ]
 
     def sum_plane(turn):
         chip = chip_at(turn)
-        to_two[turn].wait_recv()
-        own = pair_sum[turn, k_hi if turn % 2 else k_lo]
-        total = own.astype(F32) + from_two[turn].astype(F32)
+        total = chip_sum[turn, k].astype(F32)
+        for offset in range(1, blocks):
+            to_grp[turn][offset - 1].wait_recv()
+            total = total + from_grp[offset - 1, turn].astype(F32)
         if turn:
             plane_sum[turn - 1] = total.astype(BF16)
             to_z.append(
@@ -411,9 +398,9 @@
         copy.start()
         leaving.append(copy)
 
-    stages = (form, sum_cores, sum_pair, sum_plane)
-    for at in range(chips + len(stages) - 1):
-        for delay, stage in enumerate(stages):
+    stages = ((0, form), (1, sum_cores), (3, sum_plane))
+    for at in range(chips + 3):
+        for delay, stage in stages:
             if 0 <= at - delay < chips:
                 total = stage(turns[at - delay])
         if at == chips:
@@ -543,10 +530,8 @@
             pltpu.VMEM((halo_count, width), BF16),
             pltpu.VMEM((patches, part_rows, width), BF16),
             pltpu.VMEM((chips, part_rows, width), BF16),
-            pltpu.VMEM((chips, 2, 2, part_rows, LANES), BF16),
-            pltpu.VMEM((chips, 2, part_rows, LANES), BF16),
-            pltpu.VMEM((chips, 2, part_rows, LANES), BF16),
-            pltpu.VMEM((chips, part_rows, LANES), BF16),
+            pltpu.VMEM((chips, blocks, part_rows, LANES), BF16),
+            pltpu.VMEM((blocks - 1, chips, part_rows, LANES), BF16),
             pltpu.VMEM((chips - 1, part_rows, LANES), BF16),
             pltpu.VMEM((chips - 1, part_rows, LANES), BF16),
             pltpu.VMEM((part_rows, LANES), BF16),
@@ -559,7 +544,7 @@
             sems(4),
             sems(4),
             sems(chips),
-            sems(chips, 2),
+            sems(chips, blocks - 1),
             sems(chips - 1),
             sems(far),
             sems(blocks - 1),

time: 53.1 us -> 52.7 us (level)
  no operation moved by 1% of the time
where the time goes in v4:
time: 52.7 us; the launch traced here: 52.5 us
  Pallas kernels  51.9 us (98%)
  between operations  0.64 us (1%)
    pallas_call x1, Pallas kernels, on_device(): pl.pallas_call(functools.partial(kernel, groups, patches), out_shape=rows...  48.6 us
    pallas_call x1, Pallas kernels, on_device(): pl.pallas_call(functools.partial(finish, first_rows, second_rows), out_sh...  3.23 us

profile of v4, /device:TPU:0, one launch (start us, length us, event | category | flops | bytes accessed | tf_op | source)
XLA Modules:
  0.0 52.5 jit_solution(9499190782295362487)
XLA Ops:
  0.6 48.6 %shard_map.162 = (bf16[512,512]{1,0:T(8,128)(2,1)}, bf16[128,512]{1,0:T(8,128)(2,1)}, bf16[512,512]{1,0:T(8,128)(2,1)}, bf16[128,512]{1,0:T(8,128)(2,1)}, bf16[288,512]{1,0:T(8,128)(2,1)}) custom-call(s32[4]{0:T(128)} %counts_hbm.1, bf16[128,512]{1,0:T(8,128)(2,1)} %fine_hbm.1, bf16[512,512]{1,0:T(8,128)(2,1)} %edge_hbm.1, bf16[256,512]{1,0:T(8,128)(2,1)} %coarse_hbm.1, ...), custom_call_target="tpu_custom_call" | custom-call | tf_op jit(solution)/shard_map/pallas_call | solution.py:502
  49.3 3.2 %shard_map.163 = (bf16[512,512]{1,0:T(8,128)(2,1)}, bf16[128,512]{1,0:T(8,128)(2,1)}, bf16[512,512]{1,0:T(8,128)(2,1)}, bf16[128,512]{1,0:T(8,128)(2,1)}, f32[32...) custom-call(bf16[288,512]{1,0:T(8,128)(2,1)} %get-tuple-element.12.result, ...), custom_call_target="tpu_custom_call" | custom-call | tf_op jit(solution)/shard_map/pallas_call | solution.py:572
